TPU v7x, 512 devices: a whole 4x8x8 slice. The times are simulated.
512 devices in a mesh: mp: 16 (over x_lo, y), dp: 32 (over z, x_hi, core).
Axes of the slice: x: 4 (x_hi: 2, x_lo: 2; x = x_hi * 2 + x_lo), y: 8, z: 8, core: 2. Of those that a mesh axis runs over, the one named last changes fastest.
Arguments:
- grad_parts: bfloat16 [32, 128, 73728], P('dp', 'mp'), may hold values from -1200 to 1200
- param: float32 [128, 73728], P('mp', 'dp'), may hold values from -40 to 40
- row_prior: float32 [128], P('mp'), may hold values from 0.05 to 1
- col_prior: float32 [73728], P('dp'), may hold values from 0.05 to 1
Outputs:
- updated: float32 [128, 73728], P('mp', 'dp')
- row_state: float32 [128], P('mp')
- col_state: float32 [73728], P('dp')
- update_rms: float32 [], replicated
All inputs are finite; a program needn't handle non-finite values.
Results may differ from a plain program's by a relative error of at most 0.0003.
Values sent between devices are 32-bit elements; how exact they have to be, the bound alone decides.
No kernel may reach another device: no remote copies, remote signals or barrier semaphores. Data moves between devices by JAX's collectives and lax.ppermute only.
A program may use at most 64 MiB of HBM per device.

v0:
```python
import jax
import jax.numpy as jnp
from jax import lax
from jax.sharding import PartitionSpec as P

COLS = 73728


def on_device(grad_parts, param, row_prior, col_prior):
    partial_value = grad_parts[0].astype(jnp.float32)
    replicas = lax.axis_size("dp")
    row_count = partial_value.shape[0]
    all_rows = row_count * lax.axis_size("mp")
    gradient = lax.psum_scatter(partial_value, "dp", scatter_dimension=1, tiled=True) / replicas
    squares = gradient * gradient + 1e-30
    row_part = jnp.sum(squares, axis=1)
    col_part = jnp.sum(squares, axis=0)
    row_sum = lax.psum(row_part, "dp")
    col_sum = lax.psum(col_part, "mp")
    row_state = 0.9 * row_prior + 0.1 * row_sum / COLS
    col_state = 0.9 * col_prior + 0.1 * col_sum / all_rows
    row_total = lax.psum(jnp.sum(row_state), "mp") / all_rows
    update = gradient / jnp.sqrt(row_state[:, None] * col_state[None, :] / row_total)
    update_sum, param_sum = lax.psum(
        (jnp.sum(update * update), jnp.sum(param * param)), ("mp", "dp")
    )
    entries = float(all_rows * COLS)
    update_rms = jnp.sqrt(update_sum / entries)
    param_rms = jnp.sqrt(param_sum / entries + 1e-06)
    updated = param - 0.01 * param_rms * update / jnp.maximum(1.0, update_rms)
    return (updated, row_state, col_state, update_rms)


def solution(mesh):
    in_specs = (P("dp", "mp", None), P("mp", "dp"), P("mp"), P("dp"))
    out_specs = (P("mp", "dp"), P("mp"), P("dp"), P())
    return jax.shard_map(
        on_device, mesh=mesh, in_specs=in_specs, out_specs=out_specs, check_vma=False
    )
```

profile of v0, /device:TPU:1, one launch (start us, length us, event | category | flops | bytes accessed | tf_op | source)
XLA Modules:
  0.0 382.6 jit_solution(2019769233504353233)
XLA Ops:
  7.2 0.0 copy-start
  7.2 0.0 copy-start.4
  7.2 0.0 copy-start.2
  7.2 0.0 reduce-scatter.2.cloned.1.call-start
  7.2 2.8 bitcast_convert_fusion
  10.1 0.0 reduce-scatter.2.cloned.1.call-update
  10.1 0.0 copy-done
  10.1 0.6 multiply_reduce_fusion.1
  10.7 131.8 %reduce-scatter.2.cloned.1.call-done = f32[8,2304]{1,0:T(8,128)} async-done(((f32[8,73728]{1,0:T(8,128)}), f32[8,2304]{1,0:T(8,128)}) %reduce-scatter.2.cloned.1.call-update) | async-done | bytes 73744 | tf_op jit(solution)/shard_map/reduce_scatter | solution.py:14
  142.5 1.0 fusion
  143.5 70.2 %psum.36 = f32[8]{0:T(128)S(1)} all-reduce(f32[8]{0:T(128)S(1)} %get-tuple-element.5), channel_id=1, replica_groups=mesh['mp'=16,'dp'=32] {'dp'}, use_global_device_ids=true, to_apply=%region_4.0 | all-reduce | flops 8 | bytes 64 | tf_op jit(solution)/shard_map/psum | solution.py:18
  213.7 0.0 copy-done.4
  213.7 0.6 fusion.2
  214.3 0.0 copy-start.3
  214.3 48.6 %all-reduce.1 = (f32[]{:T(128)}, f32[2304]{0:T(1024)S(1)}) all-reduce(f32[]{:T(128)} %get-tuple-element.10, f32[2304]{0:T(1024)S(1)} %get-tuple-element.4), channel_id=1, replica_groups=mesh['mp'=16,'dp'=32] {'mp'}, use_global_device_ids=true, to_apply=%region_8.0 | all-reduce | flops 2305 | bytes 18440 | tf_op jit(solution)/shard_map/psum | solution.py:22
  262.9 0.0 copy-done.2
  262.9 0.0 copy-start.1
  263.6 1.6 multiply_reduce_fusion
  265.2 106.5 %all-reduce = (f32[]{:T(128)}, f32[]{:T(128)}) all-reduce(f32[]{:T(128)} %multiply_reduce_fusion, f32[]{:T(128)} %multiply_reduce_fusion.1), channel_id=1, replica_groups=mesh['mp'=16,'dp'=32] {'mp','dp'}, use_global_device_ids=true, to_apply=%region_10.0 | all-reduce | flops 2 | bytes 16 | tf_op jit(solution)/shard_map/psum | solution.py:24
  373.0 1.6 divide_subtract_fusion
  374.7 0.0 copy-done.3
  374.7 0.0 copy-done.1
  (1 shorter events, 0.0 us)
Async XLA Ops:
  7.2 2.9 copy-start
  7.2 206.6 %copy-start.4 = (f32[8]{0:T(128)S(1)}, f32[8]{0:T(128)}, u32[]{:S(2)}) copy-start(f32[8]{0:T(128)} %param.6) | copy-start | bytes 100
  7.2 255.7 %copy-start.2 = (f32[2304]{0:T(1024)S(1)}, f32[2304]{0:T(1024)}, u32[]{:S(2)}) copy-start(f32[2304]{0:T(1024)} %param.7) | copy-start | bytes 27652
  7.2 135.3 %reduce-scatter.2.cloned.1.call-start = ((), (), s32[]{:S(2)}) async-start(), calls=%async_computation.1 | async-start | bytes 2433024 | tf_op jit(solution)/shard_map/reduce_scatter | solution.py:14
  214.3 160.3 %copy-start.3 = (f32[8]{0:T(128)}, f32[8]{0:T(128)S(1)}, u32[]{:S(2)}) copy-start(f32[8]{0:T(128)S(1)} %get-tuple-element.11) | copy-start | bytes 100
  262.9 111.7 %copy-start.1 = (f32[2304]{0:T(1024)}, f32[2304]{0:T(1024)S(1)}, u32[]{:S(2)}) copy-start(f32[2304]{0:T(1024)S(1)} %multiply_add_fusion.1) | copy-start | bytes 27652
Sparse Core Ops, SparseCore 0:
  12.8 129.7 reduce-scatter.1
where the time goes:
time: 383 us
  blocking collectives  225 us (59%)
  waiting for transfers between devices  132 us (34%)
  between operations  17.2 us (4%)
  other arithmetic  8.29 us (2%)
    reduce_scatter x1, waiting for transfers between devices, on_device(): lax.psum_scatter(partial_value, 'dp', scatter_dimension=1, tiled=True)  132 us
    psum x1, blocking collectives, on_device(): lax.psum((jnp.sum(update * update), jnp.sum(param * param)), ('mp', 'dp'))  106 us
    psum x1, blocking collectives, on_device(): row_sum = lax.psum(row_part, 'dp')  70.2 us
    psum x1, blocking collectives, on_device(): row_total = lax.psum(jnp.sum(row_state), 'mp') / all_rows  48.6 us
  transfers between devices with their start and end apart: 1, of which 1 were waited for; matrix products, arithmetic and copies ran while one was open for 0% of the time, Pallas kernels for 0%

commit v1 on v0

v1 whole, which is shorter than its diff:
```python
import jax
import jax.numpy as jnp
from jax import lax
from jax.sharding import PartitionSpec as P

COLS = 73728


def everyone(value, axis, size):
    width = value.shape[0]
    sent = jnp.broadcast_to(value[None, None, :], (size, 1, width))
    return lax.all_to_all(sent, axis, 0, 0, tiled=True)


def on_device(grad_parts, param, row_prior, col_prior):
    replicas = lax.axis_size("dp")
    slabs = lax.axis_size("mp")
    rows = grad_parts.shape[1]
    own = param.shape[1]
    all_rows = rows * slabs
    pairs = replicas // 2
    core = lax.axis_index("dp") % 2

    blocks = grad_parts[0].reshape(rows, pairs, 2, own).transpose(2, 1, 0, 3)
    sent = lax.dynamic_index_in_dim(blocks, 1 - core, 0, keepdims=False).astype(jnp.float32)
    kept = lax.dynamic_index_in_dim(blocks, core, 0, keepdims=False)
    got = lax.ppermute(sent, "dp", [(i, i ^ 1) for i in range(replicas)])
    both = kept.astype(jnp.float32) + got
    same_core = [[2 * i + c for i in range(pairs)] for c in range(2)]
    parts = lax.all_to_all(both, "dp", 0, 0, tiled=True, axis_index_groups=same_core)
    gradient = jnp.sum(parts, axis=0) / replicas

    power = gradient * gradient
    squares = power + 1e-30
    col_sum = jnp.sum(everyone(jnp.sum(squares, axis=0), "mp", slabs), axis=(0, 1))
    col_state = 0.9 * col_prior + 0.1 * col_sum / all_rows

    row_part = jnp.concatenate(
        [
            jnp.sum(squares, axis=1),
            jnp.sum(power / col_state[None, :], axis=1),
            jnp.sum(param * param, axis=1),
        ]
    )
    row_part = jnp.pad(row_part, (0, 128 - 3 * rows))
    row_all = jnp.sum(everyone(row_part, "dp", replicas), axis=(0, 1))
    row_sum, scaled_sum, param_rows = (row_all[i * rows : (i + 1) * rows] for i in range(3))
    row_state = 0.9 * row_prior + 0.1 * row_sum / COLS

    last = jnp.stack([jnp.sum(row_state), jnp.sum(scaled_sum / row_state), jnp.sum(param_rows)])
    last_all = jnp.sum(everyone(jnp.pad(last, (0, 125)), "mp", slabs), axis=(0, 1))
    row_total = last_all[0] / all_rows
    entries = float(all_rows * COLS)
    update_rms = jnp.sqrt(row_total * last_all[1] / entries)
    param_rms = jnp.sqrt(last_all[2] / entries + 1e-06)
    update = gradient / jnp.sqrt(row_state[:, None] * col_state[None, :] / row_total)
    updated = param - 0.01 * param_rms * update / jnp.maximum(1.0, update_rms)
    return (updated, row_state, col_state, update_rms)


def solution(mesh):
    in_specs = (P("dp", "mp", None), P("mp", "dp"), P("mp"), P("dp"))
    out_specs = (P("mp", "dp"), P("mp"), P("dp"), P())
    return jax.shard_map(
        on_device, mesh=mesh, in_specs=in_specs, out_specs=out_specs, check_vma=False
    )
```

time: 383 us -> 101 us (0.26)
  blocking collectives: 225 us -> 79.5 us
  waiting for transfers between devices: 132 us -> 2.44 us
  between operations: 17.2 us -> 3.82 us
  starting transfers between devices: 0.04 us -> 8.79 us
    psum x3 -> x0, blocking collectives: 225 us -> none  [the longest x1 106 us: on_device(): lax.psum((jnp.sum(update * update), jnp.sum(param * param)), ('mp', 'dp'))]
    reduce_scatter x1 -> x0, waiting for transfers between devices: 132 us -> none  [on_device(): lax.psum_scatter(partial_value, 'dp', scatter_dimension=1, tiled=True)]
    all_to_all x0 -> x4, blocking collectives: none -> 79.5 us  [the longest x3 40 us: everyone(): return lax.all_to_all(sent, axis, 0, 0, tiled=True)]
    ppermute x0 -> x1, starting transfers between devices: none -> 8.79 us  [on_device(): got = lax.ppermute(sent, 'dp', [(i, i ^ 1) for i in range(replicas)])]
where the time goes in v1:
time: 101 us
  blocking collectives  79.5 us (79%)
  starting transfers between devices  8.79 us (9%)
  other arithmetic  5.38 us (5%)
  between operations  3.82 us (4%)
  waiting for transfers between devices  2.44 us (2%)
    all_to_all x3, blocking collectives, everyone(): return lax.all_to_all(sent, axis, 0, 0, tiled=True)  40 us
    all_to_all x1, blocking collectives, on_device(): lax.all_to_all(both, 'dp', 0, 0, tiled=True, axis_index_groups=same_core)  39.6 us
    ppermute x1, starting transfers between devices, on_device(): got = lax.ppermute(sent, 'dp', [(i, i ^ 1) for i in range(replicas)])  8.79 us
    ppermute x1, waiting for transfers between devices, on_device(): got = lax.ppermute(sent, 'dp', [(i, i ^ 1) for i in range(replicas)])  2.44 us
    another operation x1, other arithmetic, on_device(): jnp.stack([jnp.sum(row_state), jnp.sum(scaled_sum / row_state), jnp.sum(p...  2.06 us
  transfers between devices with their start and end apart: 1, of which 1 were waited for; matrix products, arithmetic and copies ran while one was open for 0% of the time, Pallas kernels for 0%

profile of v1, /device:TPU:1, one launch (start us, length us, event | category | flops | bytes accessed | tf_op | source)
XLA Modules:
  0.0 100.7 jit_solution(8066619823164100259)
XLA Ops:
  0.6 0.0 copy-start
  0.7 1.2 %convert_bitcast_fusion = f32[16,8,2304]{2,1,0:T(8,128)S(1)} fusion(bf16[8,16,2,2304]{3,0,2,1:T(8,128)(2,1)} %bitcast.19, s32[]{:T(128)S(6)} %select_n.16), kind=kLoop, calls=%fused_computation.1 | loop fusion | flops 294912 | bytes 1769476 | tf_op jit(solution)/shard_map/convert_element_type | solution.py:25
  1.9 8.8 %collective-permute-start = (f32[16,8,2304]{2,1,0:T(8,128)S(1)}, f32[16,8,2304]{2,1,0:T(8,128)S(1)}, u32[]{:S(2)}, u32[]{:S(2)}) collective-permute-start(f32[16,8,2304]{2,1,0:T(8,128)S(1)} %convert_bitcast_fusion), channel_id=1, source_target_pairs={{0,1},{1,0},{2,3},{3,2},{4,5},{5,4},{6,7},{7,6},{8,9},{9,8},{10,11... | collective-permute-start | bytes 3538952 | tf_op jit(solution)/shard_map/ppermute | solution.py:27
  10.7 2.4 %collective-permute-done = f32[16,8,2304]{2,1,0:T(8,128)S(1)} collective-permute-done((f32[16,8,2304]{2,1,0:T(8,128)S(1)}, f32[16,8,2304]{2,1,0:T(8,128)S(1)}, u32[]{:S(2)}, u32[]{:S(2)}) %collective-permute-start) | collective-permute-done | bytes 1179680 | tf_op jit(solution)/shard_map/ppermute | solution.py:27
  13.1 0.0 copy-done
  13.1 0.1 bitcast_add_fusion
  13.3 39.6 %all_to_all.20 = f32[16,8,2304]{2,1,0:T(8,128)S(1)} all-to-all(f32[16,8,2304]{2,1,0:T(8,128)S(1)} %bitcast_add_fusion), channel_id=1, replica_groups={{0,2,4,6,8,10,12,14,16,18,20,22,24,26,28,30},{1,3,5,7,9,11,13,15,17,19,..., dimensions={0} | all-to-all | bytes 2359296 | tf_op jit(solution)/shard_map/all_to_all | solution.py:30
  52.8 0.0 copy-start.3
  52.8 0.0 copy-start.1
  52.8 0.0 copy-start.5
  52.8 0.1 reduce_sum.99
  52.9 0.1 broadcast_in_dim.6
  53.0 14.3 %all_to_all.21 = f32[16,1,2304]{2,1,0:T(1,128)S(1)} all-to-all(f32[16,1,2304]{2,1,0:T(1,128)S(1)} %broadcast_in_dim.6), channel_id=1, replica_groups=mesh['mp'=16,'dp'=32] {'mp'}, dimensions={0} | all-to-all | bytes 294912 | tf_op jit(solution)/shard_map/all_to_all | solution.py:12
  67.3 0.1 reduce_sum.102
  67.4 0.0 copy-done.3
  67.4 0.0 copy-done.1
  67.4 0.0 copy-start.2
  67.5 0.2 add_reduce_fusion.1
  67.6 0.1 select_maximum_fusion.2
  67.7 15.5 %all_to_all.22 = f32[32,1,128]{2,1,0:T(1,128)S(1)} all-to-all(f32[32,1,128]{2,1,0:T(1,128)S(1)} %broadcast_in_dim.7), channel_id=1, replica_groups=mesh['mp'=16,'dp'=32] {'dp'}, dimensions={0} | all-to-all | bytes 32768 | tf_op jit(solution)/shard_map/all_to_all | solution.py:12
  83.2 0.0 copy-done.5
  83.2 0.8 fusion.1
  84.0 0.0 copy-start.4
  84.0 2.1 %select_maximum_fusion = f32[128]{0:T(128)S(1)} fusion(f32[1]{0:T(128)} %bitcast.8, f32[1]{0:T(128)} %bitcast.7, f32[1]{0:T(128)} %bitcast.6), kind=kLoop, calls=%fused_computation.9 | loop fusion | flops 768 | bytes 524 | tf_op jit(solution)/shard_map/stack | solution.py:50
  86.0 10.2 %all_to_all.23 = f32[16,1,128]{2,1,0:T(1,128)S(1)} all-to-all(f32[16,1,128]{2,1,0:T(1,128)S(1)} %broadcast_in_dim.8), channel_id=1, replica_groups=mesh['mp'=16,'dp'=32] {'mp'}, dimensions={0} | all-to-all | bytes 16384 | tf_op jit(solution)/shard_map/all_to_all | solution.py:12
  96.3 0.6 fusion.2
  98.8 0.7 divide_subtract_fusion
  99.6 0.0 copy-done.2
  99.6 0.0 copy-done.4
  (6 shorter events, 0.1 us)
Async XLA Ops:
  0.6 12.5 %copy-start = (bf16[1,8,73728]{2,1,0:T(8,128)(2,1)S(1)}, bf16[1,8,73728]{2,1,0:T(8,128)(2,1)}, u32[]{:S(2)}) copy-start(bf16[1,8,73728]{2,1,0:T(8,128)(2,1)} %param.4) | copy-start | bytes 3538948
  1.9 11.2 %collective-permute-start = (f32[16,8,2304]{2,1,0:T(8,128)S(1)}, f32[16,8,2304]{2,1,0:T(8,128)S(1)}, u32[]{:S(2)}, u32[]{:S(2)}) collective-permute-start(f32[16,8,2304]{2,1,0:T(8,128)S(1)} %convert_bitcast_fusion), channel_id=1, source_target_pairs={{0,1},{1,0},{2,3},{3,2},{4,5},{5,4},{6,7},{7,6},{8,9},{9,8},{10,11... | collective-permute-start | bytes 3538952 | tf_op jit(solution)/shard_map/ppermute | solution.py:27
  52.8 14.6 %copy-start.3 = (f32[2304]{0:T(1024)S(1)}, f32[2304]{0:T(1024)}, u32[]{:S(2)}) copy-start(f32[2304]{0:T(1024)} %param.7) | copy-start | bytes 27652
  52.8 14.6 %copy-start.1 = (f32[8,2304]{1,0:T(8,128)S(1)}, f32[8,2304]{1,0:T(8,128)}, u32[]{:S(2)}) copy-start(f32[8,2304]{1,0:T(8,128)} %param.5) | copy-start | bytes 221188
  52.8 30.4 %copy-start.5 = (f32[8]{0:T(128)S(1)}, f32[8]{0:T(128)}, u32[]{:S(2)}) copy-start(f32[8]{0:T(128)} %param.6) | copy-start | bytes 100
  67.4 32.1 %copy-start.2 = (f32[2304]{0:T(1024)}, f32[2304]{0:T(1024)S(1)}, u32[]{:S(2)}) copy-start(f32[2304]{0:T(1024)S(1)} %multiply_add_fusion) | copy-start | bytes 27652
  84.0 15.6 %copy-start.4 = (f32[8]{0:T(128)}, f32[8]{0:T(128)S(1)}, u32[]{:S(2)}) copy-start(f32[8]{0:T(128)S(1)} %get-tuple-element.9) | copy-start | bytes 100

commit v2 on v1

v2 whole, which is shorter than its diff:
```python
import jax
import jax.numpy as jnp
from jax import lax
from jax.sharding import PartitionSpec as P

COLS = 73728


def everyone(value, axis, size):
    sent = jnp.broadcast_to(value[None], (size, *value.shape))
    return lax.all_to_all(sent, axis, 0, 0, tiled=True)


def on_device(grad_parts, param, row_prior, col_prior):
    replicas = lax.axis_size("dp")
    slabs = lax.axis_size("mp")
    rows = grad_parts.shape[1]
    own = param.shape[1]
    all_rows = rows * slabs
    pairs = replicas // 2
    core = lax.axis_index("dp") % 2

    blocks = grad_parts[0].reshape(rows, pairs, 2, own).transpose(2, 1, 0, 3)
    sent = lax.dynamic_index_in_dim(blocks, 1 - core, 0, keepdims=False).astype(jnp.float32)
    kept = lax.dynamic_index_in_dim(blocks, core, 0, keepdims=False)
    got = lax.ppermute(sent, "dp", [(i, i ^ 1) for i in range(replicas)])
    kept, param_part = lax.optimization_barrier((kept, jnp.sum(param * param, axis=1)))
    both = kept.astype(jnp.float32) + got
    far = replicas // 8
    both = jnp.concatenate([both[4 * f + n][None] for n in range(4) for f in range(far)])
    both = both.reshape(4, far, rows, own)
    near_groups = [[8 * f + 2 * n + c for n in range(4)] for f in range(far) for c in range(2)]
    parts = lax.all_to_all(both, "dp", 0, 0, tiled=True, axis_index_groups=near_groups)
    far_groups = [[8 * f + 2 * n + c for f in range(far)] for n in range(4) for c in range(2)]
    parts = jnp.sum(parts, axis=0)
    parts = lax.all_to_all(parts, "dp", 0, 0, tiled=True, axis_index_groups=far_groups)
    gradient = jnp.sum(parts, axis=0) / replicas

    power = gradient * gradient
    squares = power + 1e-30
    col_sum = jnp.sum(everyone(jnp.sum(squares, axis=0)[None], "mp", slabs), axis=(0, 1))
    col_state = 0.9 * col_prior + 0.1 * col_sum / all_rows

    row_part = jnp.stack(
        [jnp.sum(squares, axis=1), jnp.sum(power / col_state[None, :], axis=1), param_part]
    )
    row_all = jnp.sum(everyone(row_part, "dp", replicas), axis=0)
    row_state = 0.9 * row_prior + 0.1 * row_all[0] / COLS
    last = jnp.sum(jnp.stack([row_state, row_all[1] / row_state, row_all[2]]), axis=1)
    update = gradient / jnp.sqrt(row_state[:, None] * col_state[None, :])
    last, update = lax.optimization_barrier((last, update))
    last_all = jnp.sum(everyone(jnp.broadcast_to(last[:, None], (3, rows)), "mp", slabs), axis=0)
    row_total = last_all[0] / all_rows
    entries = float(all_rows * COLS)
    update_rms = jnp.sqrt(row_total * last_all[1] / entries)
    param_rms = jnp.sqrt(last_all[2] / entries + 1e-06)
    scale = 0.01 * param_rms * jnp.sqrt(row_total) / jnp.maximum(1.0, update_rms)
    updated = param - scale[:, None] * update
    return (updated, row_state, col_state, update_rms[0])


def solution(mesh):
    in_specs = (P("dp", "mp", None), P("mp", "dp"), P("mp"), P("dp"))
    out_specs = (P("mp", "dp"), P("mp"), P("dp"), P())
    return jax.shard_map(
        on_device, mesh=mesh, in_specs=in_specs, out_specs=out_specs, check_vma=False
    )
```

time: 101 us -> 93.8 us (0.929)
  between operations: 3.82 us -> 0.91 us
  blocking collectives: 79.5 us -> 77.6 us
  other arithmetic: 5.38 us -> 3.55 us
    all_to_all x1 -> x2, blocking collectives: 39.6 us -> 34.5 us  [the longest x1 18.9 us: on_device(): lax.all_to_all(both, 'dp', 0, 0, tiled=True, axis_index_groups=near_groups)]
    all_to_all x3, blocking collectives: 40 us -> 43.1 us  [everyone(): return lax.all_to_all(sent, axis, 0, 0, tiled=True)]
    another operation x1 -> x2, other arithmetic: 2.06 us -> 0.02 us  [the longest x1 0.01 us: on_device(): jnp.stack([jnp.sum(squares, axis=1), jnp.sum(power / col_state[None, :],...]
where the time goes in v2:
time: 93.8 us; the launch traced here: 93.5 us
  blocking collectives  77.6 us (83%)
  starting transfers between devices  8.79 us (9%)
  other arithmetic  3.55 us (4%)
  waiting for transfers between devices  2.31 us (2%)
    all_to_all x3, blocking collectives, everyone(): return lax.all_to_all(sent, axis, 0, 0, tiled=True)  43.1 us
    all_to_all x1, blocking collectives, on_device(): lax.all_to_all(both, 'dp', 0, 0, tiled=True, axis_index_groups=near_groups)  18.9 us
    all_to_all x1, blocking collectives, on_device(): lax.all_to_all(parts, 'dp', 0, 0, tiled=True, axis_index_groups=far_groups)  15.6 us
    ppermute x1, starting transfers between devices, on_device(): got = lax.ppermute(sent, 'dp', [(i, i ^ 1) for i in range(replicas)])  8.79 us
    ppermute x1, waiting for transfers between devices, on_device(): got = lax.ppermute(sent, 'dp', [(i, i ^ 1) for i in range(replicas)])  2.31 us
  transfers between devices with their start and end apart: 1, of which 1 were waited for; matrix products, arithmetic and copies ran while one was open for 0% of the time, Pallas kernels for 0%

profile of v2, /device:TPU:1, one launch (start us, length us, event | category | flops | bytes accessed | tf_op | source)
XLA Modules:
  0.0 93.5 jit_solution(18096967330329744867)
XLA Ops:
  0.6 0.0 copy-start
  0.7 1.4 %convert_bitcast_fusion = (f32[16,8,2304]{2,1,0:T(8,128)S(1)}, bf16[16,8,2304]{2,1,0:T(8,128)(2,1)S(1)}) fusion(bf16[8,16,2,2304]{3,0,2,1:T(8,128)(2,1)} %bitcast.30, s32[]{:T(128)S(6)} %select_n.16, s32[]{:T(128)S(6)} %select_n.15), kind=kLoop, calls=%fused_computation | loop fusion | flops 294912 | bytes 2949128 | tf_op jit(solution)/shard_map/convert_element_type | solution.py:24
  2.1 8.8 %collective-permute-start = (f32[16,8,2304]{2,1,0:T(8,128)S(1)}, f32[16,8,2304]{2,1,0:T(8,128)S(1)}, u32[]{:S(2)}, u32[]{:S(2)}) collective-permute-start(f32[16,8,2304]{2,1,0:T(8,128)S(1)} %get-tuple-element.18), channel_id=1, source_target_pairs={{0,1},{1,0},{2,3},{3,2},{4,5},{5,4},{6,7},{7,6},{8,9},{9,8},{10,11... | collective-permute-start | bytes 3538952 | tf_op jit(solution)/shard_map/ppermute | solution.py:26
  10.9 0.0 copy-done
  10.9 0.1 multiply_reduce_fusion
  11.0 2.3 %collective-permute-done = f32[16,8,2304]{2,1,0:T(8,128)S(1)} collective-permute-done((f32[16,8,2304]{2,1,0:T(8,128)S(1)}, f32[16,8,2304]{2,1,0:T(8,128)S(1)}, u32[]{:S(2)}, u32[]{:S(2)}) %collective-permute-start) | collective-permute-done | bytes 1179680 | tf_op jit(solution)/shard_map/ppermute | solution.py:26
  13.3 0.1 convert_add_fusion
  13.7 18.9 %all_to_all.25 = f32[4,4,8,2304]{3,2,1,0:T(8,128)S(1)} all-to-all(f32[4,4,8,2304]{3,2,1,0:T(8,128)S(1)} %bitcast.29), channel_id=1, replica_groups={{0,2,4,6},{1,3,5,7},{8,10,12,14},{9,11,13,15},{16,18,20,22},{17,19,21,2..., dimensions={0} | all-to-all | bytes 2359296 | tf_op jit(solution)/shard_map/all_to_all | solution.py:33
  32.5 0.1 reduce_sum.91
  32.6 0.0 copy-start.2
  32.6 0.0 copy-start.4
  32.6 15.6 %all_to_all.26 = f32[4,8,2304]{2,1,0:T(8,128)S(1)} all-to-all(f32[4,8,2304]{2,1,0:T(8,128)S(1)} %reduce_sum.91), channel_id=1, replica_groups={{0,8,16,24},{1,9,17,25},{2,10,18,26},{3,11,19,27},{4,12,20,28},{5,13,21..., dimensions={0} | all-to-all | bytes 589824 | tf_op jit(solution)/shard_map/all_to_all | solution.py:36
  48.3 0.1 broadcast_in_dim.4
  48.4 14.2 %all_to_all.27 = f32[16,1,2304]{2,1,0:T(1,128)S(1)} all-to-all(f32[16,1,2304]{2,1,0:T(1,128)S(1)} %broadcast_in_dim.4), channel_id=1, replica_groups=mesh['mp'=16,'dp'=32] {'mp'}, dimensions={0} | all-to-all | bytes 294912 | tf_op jit(solution)/shard_map/all_to_all | solution.py:11
  62.6 0.1 reduce_sum.95
  62.7 0.0 copy-done.2
  62.7 0.0 copy-start.1
  62.7 0.2 add_reduce_fusion.1
  62.9 18.7 %all_to_all.28 = f32[32,3,8]{2,1,0:T(4,128)S(1)} all-to-all(f32[32,3,8]{2,1,0:T(4,128)S(1)} %broadcast_in_dim.5), channel_id=1, replica_groups=mesh['mp'=16,'dp'=32] {'dp'}, dimensions={0} | all-to-all | bytes 6144 | tf_op jit(solution)/shard_map/all_to_all | solution.py:11
  81.7 0.0 copy-done.4
  81.7 0.0 copy-start.3
  81.7 0.1 rsqrt_multiply_fusion
  81.8 0.1 maximum_reduce_fusion
  81.9 0.1 broadcast_in_dim_broadcast_in_dim_broadcast_in_dim.2
  82.0 10.2 %all_to_all.29 = f32[16,3,8]{2,1,0:T(4,128)S(1)} all-to-all(f32[16,3,8]{2,1,0:T(4,128)S(1)} %broadcast_in_dim_broadcast_in_dim_broadcast_in_dim.2), channel_id=1, replica_groups=mesh['mp'=16,'dp'=32] {'mp'}, dimensions={0} | all-to-all | bytes 3072 | tf_op jit(solution)/shard_map/all_to_all | solution.py:11
  92.2 0.5 fusion.1
  92.7 0.7 multiply_subtract_fusion
  93.5 0.0 copy-done.1
  93.5 0.0 copy-done.3
  (25 shorter events, 0.3 us)
Async XLA Ops:
  0.6 10.2 %copy-start = (f32[8,2304]{1,0:T(8,128)S(1)}, f32[8,2304]{1,0:T(8,128)}, u32[]{:S(2)}) copy-start(f32[8,2304]{1,0:T(8,128)} %param.5) | copy-start | bytes 221188
  2.1 11.2 %collective-permute-start = (f32[16,8,2304]{2,1,0:T(8,128)S(1)}, f32[16,8,2304]{2,1,0:T(8,128)S(1)}, u32[]{:S(2)}, u32[]{:S(2)}) collective-permute-start(f32[16,8,2304]{2,1,0:T(8,128)S(1)} %get-tuple-element.18), channel_id=1, source_target_pairs={{0,1},{1,0},{2,3},{3,2},{4,5},{5,4},{6,7},{7,6},{8,9},{9,8},{10,11... | collective-permute-start | bytes 3538952 | tf_op jit(solution)/shard_map/ppermute | solution.py:26
  32.6 30.0 %copy-start.2 = (f32[2304]{0:T(1024)S(1)}, f32[2304]{0:T(1024)}, u32[]{:S(2)}) copy-start(f32[2304]{0:T(1024)} %param.7) | copy-start | bytes 27652
  32.6 49.1 %copy-start.4 = (f32[8]{0:T(128)S(1)}, f32[8]{0:T(128)}, u32[]{:S(2)}) copy-start(f32[8]{0:T(128)} %param.6) | copy-start | bytes 100
  62.7 30.8 %copy-start.1 = (f32[2304]{0:T(1024)}, f32[2304]{0:T(1024)S(1)}, u32[]{:S(2)}) copy-start(f32[2304]{0:T(1024)S(1)} %multiply_add_fusion) | copy-start | bytes 27652
  81.7 11.7 %copy-start.3 = (f32[8]{0:T(128)}, f32[8]{0:T(128)S(1)}, u32[]{:S(2)}) copy-start(f32[8]{0:T(128)S(1)} %get-tuple-element.17) | copy-start | bytes 100

commit v3 on v2

v3 whole, which is shorter than its diff:
```python
import jax
import jax.numpy as jnp
from jax import lax
from jax.sharding import PartitionSpec as P

COLS = 73728


def everyone(value, axis, size):
    sent = jnp.broadcast_to(value[None], (size, *value.shape))
    return lax.all_to_all(sent, axis, 0, 0, tiled=True)


def on_device(grad_parts, param, row_prior, col_prior):
    replicas = lax.axis_size("dp")
    slabs = lax.axis_size("mp")
    rows = grad_parts.shape[1]
    own = param.shape[1]
    all_rows = rows * slabs
    pairs = replicas // 2
    core = lax.axis_index("dp") % 2

    blocks = grad_parts[0].reshape(rows, pairs, 2, own).transpose(2, 1, 0, 3)
    sent = lax.dynamic_index_in_dim(blocks, 1 - core, 0, keepdims=False).astype(jnp.float32)
    kept = lax.dynamic_index_in_dim(blocks, core, 0, keepdims=False)
    got = lax.ppermute(sent, "dp", [(i, i ^ 1) for i in range(replicas)])
    lanes = 128
    wide = slabs * lanes
    rest = (own - wide) // slabs
    slab = lax.axis_index("mp")
    first_row = (slab * rows).astype(jnp.uint32)
    old_part = lax.optimization_barrier(0.9 * col_prior)
    tile_old = lax.dynamic_slice(old_part, ((slab * lanes).astype(jnp.uint32),), (lanes,))
    rest_old = lax.dynamic_slice(old_part, ((wide + slab * rest).astype(jnp.uint32),), (rest,))
    own_rows = jnp.arange(all_rows) // rows == slab
    priors = jnp.where(own_rows, jnp.tile(row_prior, slabs), 0.0)
    param_part = jnp.sum(param * param, axis=1)
    got, param_part, priors, tile_old, rest_old, first_row = lax.optimization_barrier(
        (got, param_part, priors, tile_old, rest_old, first_row)
    )
    both = kept.astype(jnp.float32) + got
    far = replicas // 8
    both = jnp.concatenate([both[4 * f + n][None] for n in range(4) for f in range(far)])
    both = both.reshape(4, far, rows, own)
    near_groups = [[8 * f + 2 * n + c for n in range(4)] for f in range(far) for c in range(2)]
    parts = lax.all_to_all(both, "dp", 0, 0, tiled=True, axis_index_groups=near_groups)
    parts = jnp.sum(parts, axis=0)

    piece = rows * (lanes + rest)
    main = parts[:, :, :wide].reshape(far, rows, slabs, lanes).transpose(0, 2, 1, 3)
    side = parts[:, :, wide:].reshape(far, rows, slabs, rest).transpose(0, 2, 1, 3)
    sent = jnp.concatenate(
        [main.reshape(far * slabs, 1, rows * lanes), side.reshape(far * slabs, 1, rows * rest)],
        axis=2,
    )
    all_groups = [
        [m * replicas + 8 * f + 2 * n + c for f in range(far) for m in range(slabs)]
        for n in range(4)
        for c in range(2)
    ]
    parts = lax.all_to_all(sent, ("mp", "dp"), 0, 0, tiled=True, axis_index_groups=all_groups)
    gradient = jnp.sum(parts.reshape(far, slabs, 1, piece), axis=0) / replicas

    power = gradient * gradient
    squares = power + 1e-30
    cut = rows * lanes

    def halves(value):
        value = value[:, 0]
        return value[:, :cut].reshape(slabs, rows, lanes), value[:, cut:].reshape(slabs, rows, rest)

    cols = [
        old + 0.1 * jnp.sum(value, axis=(0, 1)) / all_rows
        for old, value in zip((tile_old, rest_old), halves(squares))
    ]

    def along_rows(tile_value, rest_value):
        gap = lanes - rest
        return jnp.sum(tile_value + jnp.pad(rest_value, ((0, 0), (0, 0), (0, gap))), axis=2)

    row_part = along_rows(*halves(squares))
    scaled_part = along_rows(*(value / c for value, c in zip(halves(power), cols)))
    sums = jnp.concatenate(
        [
            jnp.stack([row_part, scaled_part]).reshape(2 * all_rows),
            jnp.pad(param_part, (0, all_rows - rows)),
        ]
    )[None]
    known = jnp.concatenate([jnp.pad(jnp.concatenate(cols), (0, 2 * lanes - lanes - rest)), priors])
    known = jnp.broadcast_to(known, (slabs, 1, 2 * lanes + all_rows))
    known = jnp.concatenate([gradient, known], axis=2)
    sums, known = lax.optimization_barrier((sums, known))
    sums = jnp.sum(everyone(sums, "dp", replicas), axis=0)

    known = jnp.concatenate([known, jnp.broadcast_to(sums, (slabs, *sums.shape))], axis=2)
    known = lax.all_to_all(known, "mp", 0, 0, tiled=True)
    at = piece + 2 * lanes
    priors = jnp.sum(known[:, 0, at : at + all_rows], axis=0)
    sums = jnp.sum(known[:, 0, at + all_rows :], axis=0)
    row_sum, scaled_sum, param_sum = (sums[i * all_rows : (i + 1) * all_rows] for i in range(3))
    row_states = 0.9 * priors + 0.1 * row_sum / COLS
    totals = jnp.stack([row_states, scaled_sum / row_states, param_sum])
    totals = lax.optimization_barrier(jnp.broadcast_to(totals[:, None, :], (3, rows, all_rows)))
    totals = jnp.sum(totals, axis=2)
    row_state = lax.dynamic_slice(row_states, (first_row,), (rows,))
    main, side = halves(known[:, :, :piece])
    gradient = jnp.concatenate(
        [
            main.transpose(1, 0, 2).reshape(rows, wide),
            side.transpose(1, 0, 2).reshape(rows, own - wide),
        ],
        axis=1,
    )
    col_state = jnp.concatenate(
        [
            known[:, 0, piece : piece + lanes].reshape(wide),
            known[:, 0, piece + lanes : piece + lanes + rest].reshape(own - wide),
        ]
    )
    row_total = totals[0] / all_rows
    entries = float(all_rows * COLS)
    update_rms = jnp.sqrt(row_total * totals[1] / entries)
    param_rms = jnp.sqrt(totals[2] / entries + 1e-06)
    scale = 0.01 * param_rms * jnp.sqrt(row_total) / jnp.maximum(1.0, update_rms)
    update = gradient / jnp.sqrt(row_state[:, None] * col_state[None, :])
    updated = param - scale[:, None] * update
    return (updated, row_state, col_state, update_rms[0])


def solution(mesh):
    in_specs = (P("dp", "mp", None), P("mp", "dp"), P("mp"), P("dp"))
    out_specs = (P("mp", "dp"), P("mp"), P("dp"), P())
    return jax.shard_map(
        on_device, mesh=mesh, in_specs=in_specs, out_specs=out_specs, check_vma=False
    )
```

time: 93.8 us -> 90.5 us (0.965)
  blocking collectives: 77.6 us -> 72.2 us
  waiting for transfers between devices: 2.31 us -> 0.01 us
  local copies, waits for them, and re-layouts: 0.33 us -> 2.35 us
  other arithmetic: 3.55 us -> 5.48 us
    all_to_all x3 -> x1, blocking collectives: 43.1 us -> 17.5 us  [everyone(): return lax.all_to_all(sent, axis, 0, 0, tiled=True)]
    all_to_all x1 -> x2, blocking collectives: 15.6 us -> 35.7 us  [the longest x1 25.7 us: on_device(): lax.all_to_all(sent, ('mp', 'dp'), 0, 0, tiled=True, axis_index_groups=al...]
    ppermute x1, waiting for transfers between devices: 2.31 us -> 0.01 us  [on_device(): got = lax.ppermute(sent, 'dp', [(i, i ^ 1) for i in range(replicas)])]
  transfers between devices with their start and end apart: 1 -> 1, of which waited for: 1 -> 0; matrix products, arithmetic and copies ran while one was open for 0% -> 3% of each run, Pallas kernels for 0% -> 0%
where the time goes in v3:
time: 90.5 us; the launch traced here: 90 us
  blocking collectives  72.2 us (80%)
  starting transfers between devices  8.79 us (10%)
  other arithmetic  5.48 us (6%)
  local copies, waits for them, and re-layouts  2.35 us (3%)
  between operations  1.2 us (1%)
    all_to_all x1, blocking collectives, on_device(): lax.all_to_all(sent, ('mp', 'dp'), 0, 0, tiled=True, axis_index_groups=al...  25.7 us
    all_to_all x1, blocking collectives, on_device(): lax.all_to_all(both, 'dp', 0, 0, tiled=True, axis_index_groups=near_groups)  19 us
    all_to_all x1, blocking collectives, everyone(): return lax.all_to_all(sent, axis, 0, 0, tiled=True)  17.5 us
    all_to_all x1, blocking collectives, on_device(): known = lax.all_to_all(known, 'mp', 0, 0, tiled=True)  10 us
    ppermute x1, starting transfers between devices, on_device(): got = lax.ppermute(sent, 'dp', [(i, i ^ 1) for i in range(replicas)])  8.79 us
  transfers between devices with their start and end apart: 1, of which 0 were waited for; matrix products, arithmetic and copies ran while one was open for 3% of the time, Pallas kernels for 0%

profile of v3, /device:TPU:1, one launch (start us, length us, event | category | flops | bytes accessed | tf_op | source)
XLA Modules:
  0.0 90.0 jit_solution(8671150895993434539)
XLA Ops:
  0.7 1.2 %convert_bitcast_fusion = f32[16,8,2304]{2,1,0:T(8,128)S(1)} fusion(bf16[8,16,2,2304]{3,0,2,1:T(8,128)(2,1)} %bitcast.56, s32[]{:T(128)S(6)} %select_n.25), kind=kLoop, calls=%fused_computation.1 | loop fusion | flops 294912 | bytes 1769476 | tf_op jit(solution)/shard_map/convert_element_type | solution.py:24
  1.9 8.8 %collective-permute-start = (f32[16,8,2304]{2,1,0:T(8,128)S(1)}, f32[16,8,2304]{2,1,0:T(8,128)S(1)}, u32[]{:S(2)}, u32[]{:S(2)}) collective-permute-start(f32[16,8,2304]{2,1,0:T(8,128)S(1)} %convert_bitcast_fusion), channel_id=1, source_target_pairs={{0,1},{1,0},{2,3},{3,2},{4,5},{5,4},{6,7},{7,6},{8,9},{9,8},{10,11... | collective-permute-start | bytes 3538952 | tf_op jit(solution)/shard_map/ppermute | solution.py:26
  10.7 0.1 tile.10
  10.8 0.7 broadcast_multiply_fusion.1
  11.5 0.1 dynamic_slice.19
  11.6 0.6 dynamic_slice.18
  12.2 1.0 %multiply_reduce_fusion = f32[8]{0:T(128)S(1)} fusion(f32[8,2304]{1,0:T(8,128)} %param.5), kind=kLoop, calls=%fused_computation.25 | loop fusion | flops 36856 | bytes 73760 | tf_op jit(solution)/shard_map/reduce_sum | solution.py:37
  13.2 0.1 bitcast_add_fusion
  13.6 19.0 %all_to_all.20 = f32[4,4,8,2304]{3,2,1,0:T(8,128)S(1)} all-to-all(f32[4,4,8,2304]{3,2,1,0:T(8,128)S(1)} %bitcast.54), channel_id=1, replica_groups={{0,2,4,6},{1,3,5,7},{8,10,12,14},{9,11,13,15},{16,18,20,22},{17,19,21,2..., dimensions={0} | all-to-all | bytes 2359296 | tf_op jit(solution)/shard_map/all_to_all | solution.py:46
  32.6 0.1 reduce_sum.114
  32.7 0.1 reshape.133
  32.8 0.1 copy.30
  32.9 0.1 reshape.134
  33.1 0.3 pad_maximum_fusion
  33.3 25.7 %all_to_all.21 = f32[64,1,1152]{2,1,0:T(1,128)S(1)} all-to-all(f32[64,1,1152]{2,1,0:T(1,128)S(1)} %pad_maximum_fusion), channel_id=1, replica_groups={{0,32,64,96,128,160,192,224,256,288,320,352,384,416,448,480,8,40,72,104..., dimensions={0} | all-to-all | bytes 589824 | tf_op jit(solution)/shard_map/all_to_all | solution.py:61
  59.3 0.1 reduce_sum.121
  59.4 0.1 reshape.137
  59.5 0.1 add_reduce_fusion.1
  59.7 0.1 reshape.139
  59.8 0.1 add_reduce_fusion
  60.0 0.1 copy.34
  60.1 0.1 reshape.140
  60.2 0.1 pad_maximum_fusion.2
  60.3 17.5 %all_to_all.22 = f32[32,1,384]{2,1,0:T(1,128)S(1)} all-to-all(f32[32,1,384]{2,1,0:T(1,128)S(1)} %broadcast_in_dim.36), channel_id=1, replica_groups=mesh['mp'=16,'dp'=32] {'dp'}, dimensions={0} | all-to-all | bytes 98304 | tf_op jit(solution)/shard_map/all_to_all | solution.py:11
  77.9 0.1 pad_maximum_fusion.1
  78.0 10.0 %all_to_all.23 = f32[16,1,1920]{2,1,0:T(1,128)S(1)} all-to-all(f32[16,1,1920]{2,1,0:T(1,128)S(1)} %pad_maximum_fusion.1), channel_id=1, replica_groups=mesh['mp'=16,'dp'=32] {'mp'}, dimensions={0} | all-to-all | bytes 245760 | tf_op jit(solution)/shard_map/all_to_all | solution.py:96
  88.1 0.1 reshape_squeeze.11
  88.3 0.1 dynamic_slice.20
  88.4 0.1 reduce_sum.127
  88.5 0.5 fusion.3
  89.1 0.1 reshape.144
  89.2 0.7 fusion.1
  (74 shorter events, 1.0 us)
Async XLA Ops:
  0.6 12.6 %copy-start = (bf16[1,8,73728]{2,1,0:T(8,128)(2,1)S(1)}, bf16[1,8,73728]{2,1,0:T(8,128)(2,1)}, u32[]{:S(2)}) copy-start(bf16[1,8,73728]{2,1,0:T(8,128)(2,1)} %param.4) | copy-start | bytes 3538948
  0.6 10.1 %copy-start.4 = (f32[8]{0:T(128)S(1)}, f32[8]{0:T(128)}, u32[]{:S(2)}) copy-start(f32[8]{0:T(128)} %param.6) | copy-start | bytes 100
  1.9 11.3 %collective-permute-start = (f32[16,8,2304]{2,1,0:T(8,128)S(1)}, f32[16,8,2304]{2,1,0:T(8,128)S(1)}, u32[]{:S(2)}, u32[]{:S(2)}) collective-permute-start(f32[16,8,2304]{2,1,0:T(8,128)S(1)} %convert_bitcast_fusion), channel_id=1, source_target_pairs={{0,1},{1,0},{2,3},{3,2},{4,5},{5,4},{6,7},{7,6},{8,9},{9,8},{10,11... | collective-permute-start | bytes 3538952 | tf_op jit(solution)/shard_map/ppermute | solution.py:26
  33.3 26.1 %copy-start.5 = (f32[128]{0:T(128)S(1)}, f32[128]{0:T(128)}, u32[]{:S(2)}) copy-start(f32[128]{0:T(128)} %dynamic_slice.18) | copy-start | bytes 1540
  59.6 29.6 %copy-start.1 = (f32[8,2304]{1,0:T(8,128)S(1)}, f32[8,2304]{1,0:T(8,128)}, u32[]{:S(2)}) copy-start(f32[8,2304]{1,0:T(8,128)} %param.5) | copy-start | bytes 221188
  88.4 1.6 %copy-start.3 = (f32[8]{0:T(128)}, f32[8]{0:T(128)S(1)}, u32[]{:S(2)}) copy-start(f32[8]{0:T(128)S(1)} %dynamic_slice.20) | copy-start | bytes 100
  89.2 0.8 copy-start.2

commit v4 on v3

v4 whole, which is shorter than its diff:
```python
import jax
import jax.numpy as jnp
from jax import lax
from jax.sharding import PartitionSpec as P

COLS = 73728
LANES = 128


def everyone(value, axis, size):
    sent = jnp.broadcast_to(value[None], (size, *value.shape))
    return lax.all_to_all(sent, axis, 0, 0, tiled=True)


def on_device(grad_parts, param, row_prior, col_prior):
    replicas = lax.axis_size("dp")
    slabs = lax.axis_size("mp")
    rows = grad_parts.shape[1]
    own = param.shape[1]
    all_rows = rows * slabs
    pairs = replicas // 2
    core = lax.axis_index("dp") % 2
    far, near, wide = replicas // 8, 4, 2
    deep = slabs // wide
    half = own // wide
    tiles = deep * LANES
    rest = (half - tiles) // deep
    slab = lax.axis_index("mp")
    across, along = slab // deep, slab % deep

    def device(f, n, c, x, y):
        return (deep * x + y) * replicas + 8 * f + 2 * n + c

    blocks = grad_parts[0].reshape(rows, pairs, 2, own).transpose(2, 1, 0, 3)
    sent = lax.dynamic_index_in_dim(blocks, 1 - core, 0, keepdims=False).astype(jnp.float32)
    kept = lax.dynamic_index_in_dim(blocks, core, 0, keepdims=False)
    got = lax.ppermute(sent, "dp", [(i, i ^ 1) for i in range(replicas)])
    place = wide * along + across
    first_row = (place * rows).astype(jnp.uint32)
    old_part = lax.optimization_barrier(0.9 * col_prior)
    tile_at = half * across + LANES * along
    rest_at = half * across + tiles + rest * along
    tile_old = lax.dynamic_slice(old_part, (tile_at.astype(jnp.uint32),), (LANES,))
    rest_old = lax.dynamic_slice(old_part, (rest_at.astype(jnp.uint32),), (rest,))
    priors = jnp.where(jnp.arange(all_rows) // rows == place, jnp.tile(row_prior, slabs), 0.0)
    param_part = jnp.sum(param * param, axis=1)
    got, param_part, priors, tile_old, rest_old, first_row = lax.optimization_barrier(
        (got, param_part, priors, tile_old, rest_old, first_row)
    )
    both = kept.astype(jnp.float32) + got

    both = jnp.concatenate(
        [
            both[near * f + n, :, half * x : half * (x + 1)][None]
            for n in range(near)
            for x in range(wide)
            for f in range(far)
        ]
    ).reshape(near * wide, far, rows, half)
    near_groups = [
        [device(f, n, c, x, y) for n in range(near) for x in range(wide)]
        for f in range(far)
        for c in range(2)
        for y in range(deep)
    ]
    parts = lax.all_to_all(both, ("mp", "dp"), 0, 0, tiled=True, axis_index_groups=near_groups)
    parts = jnp.sum(parts.reshape(near, wide, far, rows, half), axis=0)

    main = parts[..., :tiles].reshape(wide, far, rows, deep, LANES).transpose(1, 3, 0, 2, 4)
    side = parts[..., tiles:].reshape(wide, far, rows, deep, rest).transpose(1, 3, 0, 2, 4)
    cut = rows * LANES
    piece = cut + rows * rest
    sent = jnp.concatenate(
        [
            main.reshape(far * deep, 1, wide * cut),
            side.reshape(far * deep, 1, wide * rows * rest),
        ],
        axis=2,
    )
    far_groups = [
        [device(f, n, c, x, y) for f in range(far) for y in range(deep)]
        for n in range(near)
        for c in range(2)
        for x in range(wide)
    ]
    parts = lax.all_to_all(sent, ("mp", "dp"), 0, 0, tiled=True, axis_index_groups=far_groups)
    gradient = jnp.sum(parts.reshape(far, deep, 1, wide * piece), axis=0) / replicas

    flat = gradient[:, 0]
    halves = (
        flat[:, : wide * cut].reshape(slabs, rows, LANES),
        flat[:, wide * cut :].reshape(slabs, rows, rest),
    )
    power = [value * value for value in halves]
    squares = [value + 1e-30 for value in power]
    cols = [
        old + 0.1 * jnp.sum(value, axis=(0, 1)) / all_rows
        for old, value in zip((tile_old, rest_old), squares)
    ]

    def along_rows(tile_value, rest_value):
        gap = LANES - rest
        return jnp.sum(tile_value + jnp.pad(rest_value, ((0, 0), (0, 0), (0, gap))), axis=2)

    row_part = along_rows(*squares)
    scaled_part = along_rows(*(value / c for value, c in zip(power, cols)))
    sums = jnp.concatenate(
        [
            jnp.stack([row_part, scaled_part]).reshape(2 * all_rows),
            jnp.pad(param_part, (0, all_rows - rows)),
        ]
    )[None]
    known = jnp.concatenate([jnp.pad(jnp.concatenate(cols), (0, LANES - rest)), priors])
    known = jnp.broadcast_to(known, (slabs, 1, 2 * LANES + all_rows))
    main = gradient[:, 0, : wide * cut].reshape(deep, wide, cut).transpose(1, 0, 2)
    side = gradient[:, 0, wide * cut :].reshape(deep, wide, piece - cut).transpose(1, 0, 2)
    known = jnp.concatenate(
        [main.reshape(slabs, 1, cut), side.reshape(slabs, 1, piece - cut), known], axis=2
    )
    sums, known = lax.optimization_barrier((sums, known))
    sums = jnp.sum(everyone(sums, "dp", replicas), axis=0)

    known = jnp.concatenate([known, jnp.broadcast_to(sums, (slabs, *sums.shape))], axis=2)
    known = lax.all_to_all(known, "mp", 0, 0, tiled=True)
    at = piece + 2 * LANES
    priors = jnp.sum(known[:, 0, at : at + all_rows], axis=0)
    sums = jnp.sum(known[:, 0, at + all_rows :], axis=0)
    row_sum, scaled_sum, param_sum = (sums[i * all_rows : (i + 1) * all_rows] for i in range(3))
    row_states = 0.9 * priors + 0.1 * row_sum / COLS
    totals = jnp.stack([row_states, scaled_sum / row_states, param_sum])
    totals = lax.optimization_barrier(jnp.broadcast_to(totals[:, None, :], (3, rows, all_rows)))
    totals = jnp.sum(totals, axis=2)
    row_state = lax.dynamic_slice(row_states, (first_row,), (rows,))

    def in_columns(start, width, lines):
        value = known[:, 0, start : start + lines * width].reshape(slabs, lines, width)
        value = value.transpose(1, 0, 2).reshape(lines, wide, deep * width)
        return [value[:, x] for x in range(wide)]

    def whole(start, lines):
        tile_value = in_columns(start, LANES, lines)
        rest_value = in_columns(start + lines * LANES, rest, lines)
        return jnp.concatenate(
            [v for pair in zip(tile_value, rest_value) for v in pair], axis=1
        )

    gradient = whole(0, rows)
    col_state = whole(piece, 1)[0]
    row_total = totals[0] / all_rows
    entries = float(all_rows * COLS)
    update_rms = jnp.sqrt(row_total * totals[1] / entries)
    param_rms = jnp.sqrt(totals[2] / entries + 1e-06)
    scale = 0.01 * param_rms * jnp.sqrt(row_total) / jnp.maximum(1.0, update_rms)
    update = gradient / jnp.sqrt(row_state[:, None] * col_state[None, :])
    updated = param - scale[:, None] * update
    return (updated, row_state, col_state, update_rms[0])


def solution(mesh):
    in_specs = (P("dp", "mp", None), P("mp", "dp"), P("mp"), P("dp"))
    out_specs = (P("mp", "dp"), P("mp"), P("dp"), P())
    return jax.shard_map(
        on_device, mesh=mesh, in_specs=in_specs, out_specs=out_specs, check_vma=False
    )
```

time: 90.5 us -> 90.1 us (level)
    all_to_all x1, blocking collectives: 10 us -> 11.1 us  [on_device(): known = lax.all_to_all(known, 'mp', 0, 0, tiled=True)]
    all_to_all x2, blocking collectives: 44.7 us -> 43.5 us  [the longest x1 24.8 us: on_device(): lax.all_to_all(sent, ('mp', 'dp'), 0, 0, tiled=True, axis_index_groups=fa...]
where the time goes in v4:
time: 90.1 us; the launch traced here: 89.5 us
  blocking collectives  71.5 us (79%)
  starting transfers between devices  8.79 us (10%)
  other arithmetic  5.26 us (6%)
  local copies, waits for them, and re-layouts  2.6 us (3%)
  between operations  1.32 us (1%)
    all_to_all x1, blocking collectives, on_device(): lax.all_to_all(sent, ('mp', 'dp'), 0, 0, tiled=True, axis_index_groups=fa...  24.8 us
    all_to_all x1, blocking collectives, on_device(): lax.all_to_all(both, ('mp', 'dp'), 0, 0, tiled=True, axis_index_groups=ne...  18.8 us
    all_to_all x1, blocking collectives, everyone(): return lax.all_to_all(sent, axis, 0, 0, tiled=True)  16.8 us
    all_to_all x1, blocking collectives, on_device(): known = lax.all_to_all(known, 'mp', 0, 0, tiled=True)  11.1 us
    ppermute x1, starting transfers between devices, on_device(): got = lax.ppermute(sent, 'dp', [(i, i ^ 1) for i in range(replicas)])  8.79 us
  transfers between devices with their start and end apart: 1, of which 0 were waited for; matrix products, arithmetic and copies ran while one was open for 3% of the time, Pallas kernels for 0%

profile of v4, /device:TPU:1, one launch (start us, length us, event | category | flops | bytes accessed | tf_op | source)
XLA Modules:
  0.0 89.5 jit_solution(15746911641040471514)
XLA Ops:
  0.7 1.2 %convert_bitcast_fusion = f32[16,8,2304]{2,1,0:T(8,128)S(1)} fusion(bf16[8,16,2,2304]{3,0,2,1:T(8,128)(2,1)} %bitcast.75, s32[]{:T(128)S(6)} %select_n.33), kind=kLoop, calls=%fused_computation.1 | loop fusion | flops 294912 | bytes 1769476 | tf_op jit(solution)/shard_map/convert_element_type | solution.py:35
  1.9 8.8 %collective-permute-start = (f32[16,8,2304]{2,1,0:T(8,128)S(1)}, f32[16,8,2304]{2,1,0:T(8,128)S(1)}, u32[]{:S(2)}, u32[]{:S(2)}) collective-permute-start(f32[16,8,2304]{2,1,0:T(8,128)S(1)} %convert_bitcast_fusion), channel_id=1, source_target_pairs={{0,1},{1,0},{2,3},{3,2},{4,5},{5,4},{6,7},{7,6},{8,9},{9,8},{10,11... | collective-permute-start | bytes 3538952 | tf_op jit(solution)/shard_map/ppermute | solution.py:37
  10.8 0.1 tile.10
  10.8 0.7 broadcast_multiply_fusion.1
  11.6 0.6 dynamic_slice.19
  12.1 0.1 dynamic_slice.18
  12.2 1.0 %multiply_reduce_fusion = f32[8]{0:T(128)S(1)} fusion(f32[8,2304]{1,0:T(8,128)} %param.5), kind=kLoop, calls=%fused_computation.9 | loop fusion | flops 36856 | bytes 73760 | tf_op jit(solution)/shard_map/reduce_sum | solution.py:46
  13.3 0.1 bitcast_add_fusion
  13.8 18.8 %all_to_all.20 = f32[8,4,8,1152]{3,2,1,0:T(8,128)S(1)} all-to-all(f32[8,4,8,1152]{3,2,1,0:T(8,128)S(1)} %bitcast.74), channel_id=1, replica_groups={{0,256,2,258,4,260,6,262},{32,288,34,290,36,292,38,294},{64,320,66,322,..., dimensions={0} | all-to-all | bytes 2359296 | tf_op jit(solution)/shard_map/all_to_all | solution.py:66
  32.6 0.1 reduce_sum.100
  32.8 0.1 reshape.120
  32.9 0.1 reshape.121
  33.1 0.3 copy.33
  33.4 24.8 %all_to_all.21 = f32[32,1,2304]{2,1,0:T(1,128)S(1)} all-to-all(f32[32,1,2304]{2,1,0:T(1,128)S(1)} %copy.33), channel_id=1, replica_groups={{0,32,64,96,128,160,192,224,8,40,72,104,136,168,200,232,16,48,80,112,14..., dimensions={0} | all-to-all | bytes 589824 | tf_op jit(solution)/shard_map/all_to_all | solution.py:86
  58.3 0.1 reshape.124
  58.4 0.1 mul.97
  58.6 0.1 add_reduce_fusion.1
  58.7 0.1 copy.34
  58.8 0.1 add_reduce_fusion
  59.0 0.1 copy.36
  59.0 0.1 reshape.123
  59.2 0.1 maximum_maximum_fusion
  59.3 16.8 %all_to_all.22 = f32[32,1,384]{2,1,0:T(1,128)S(1)} all-to-all(f32[32,1,384]{2,1,0:T(1,128)S(1)} %broadcast_in_dim.35), channel_id=1, replica_groups=mesh['mp'=16,'dp'=32] {'dp'}, dimensions={0} | all-to-all | bytes 98304 | tf_op jit(solution)/shard_map/all_to_all | solution.py:12
  76.2 0.1 pad_maximum_fusion.1
  76.3 11.1 %all_to_all.23 = f32[16,1,1920]{2,1,0:T(1,128)S(1)} all-to-all(f32[16,1,1920]{2,1,0:T(1,128)S(1)} %pad_maximum_fusion.1), channel_id=1, replica_groups=mesh['mp'=16,'dp'=32] {'mp'}, dimensions={0} | all-to-all | bytes 245760 | tf_op jit(solution)/shard_map/all_to_all | solution.py:124
  87.5 0.1 reshape_transpose_reshape_squeeze.7
  87.7 0.1 dynamic_slice.20
  87.8 0.1 reduce_sum.109
  87.9 0.5 fusion.3
  88.5 0.1 reshape_squeeze.19
  88.6 0.1 reshape.127
  88.7 0.7 fusion.1
  (88 shorter events, 0.9 us)
Async XLA Ops:
  0.6 12.6 %copy-start = (bf16[1,8,73728]{2,1,0:T(8,128)(2,1)S(1)}, bf16[1,8,73728]{2,1,0:T(8,128)(2,1)}, u32[]{:S(2)}) copy-start(bf16[1,8,73728]{2,1,0:T(8,128)(2,1)} %param.4) | copy-start | bytes 3538948
  0.6 10.1 %copy-start.4 = (f32[8]{0:T(128)S(1)}, f32[8]{0:T(128)}, u32[]{:S(2)}) copy-start(f32[8]{0:T(128)} %param.6) | copy-start | bytes 100
  1.9 11.3 %collective-permute-start = (f32[16,8,2304]{2,1,0:T(8,128)S(1)}, f32[16,8,2304]{2,1,0:T(8,128)S(1)}, u32[]{:S(2)}, u32[]{:S(2)}) collective-permute-start(f32[16,8,2304]{2,1,0:T(8,128)S(1)} %convert_bitcast_fusion), channel_id=1, source_target_pairs={{0,1},{1,0},{2,3},{3,2},{4,5},{5,4},{6,7},{7,6},{8,9},{9,8},{10,11... | collective-permute-start | bytes 3538952 | tf_op jit(solution)/shard_map/ppermute | solution.py:37
  33.1 25.4 %copy-start.5 = (f32[16]{0:T(128)S(1)}, f32[16]{0:T(128)}, u32[]{:S(2)}) copy-start(f32[16]{0:T(128)} %dynamic_slice.19) | copy-start | bytes 196
  58.4 30.3 %copy-start.1 = (f32[8,2304]{1,0:T(8,128)S(1)}, f32[8,2304]{1,0:T(8,128)}, u32[]{:S(2)}) copy-start(f32[8,2304]{1,0:T(8,128)} %param.5) | copy-start | bytes 221188
  87.8 1.6 %copy-start.3 = (f32[8]{0:T(128)}, f32[8]{0:T(128)S(1)}, u32[]{:S(2)}) copy-start(f32[8]{0:T(128)S(1)} %dynamic_slice.20) | copy-start | bytes 100
  88.7 0.8 copy-start.2

commit v5 on v4

--- a/solution.py
+++ b/solution.py
@@ -42,20 +42,17 @@
     rest_at = half * across + tiles + rest * along
     tile_old = lax.dynamic_slice(old_part, (tile_at.astype(jnp.uint32),), (LANES,))
     rest_old = lax.dynamic_slice(old_part, (rest_at.astype(jnp.uint32),), (rest,))
-    priors = jnp.where(jnp.arange(all_rows) // rows == place, jnp.tile(row_prior, slabs), 0.0)
+    own_slab = jnp.arange(slabs)[:, None] == place
+    old_rows = jnp.where(own_slab, (0.9 * row_prior / replicas)[None, :], 0.0)
     param_part = jnp.sum(param * param, axis=1)
-    got, param_part, priors, tile_old, rest_old, first_row = lax.optimization_barrier(
-        (got, param_part, priors, tile_old, rest_old, first_row)
+    got, param_part, old_rows, tile_old, rest_old, first_row = lax.optimization_barrier(
+        (got, param_part, old_rows, tile_old, rest_old, first_row)
     )
     both = kept.astype(jnp.float32) + got
 
+    both = both.reshape(far, near, rows, own)
     both = jnp.concatenate(
-        [
-            both[near * f + n, :, half * x : half * (x + 1)][None]
-            for n in range(near)
-            for x in range(wide)
-            for f in range(far)
-        ]
+        [both[:, n, :, half * x : half * (x + 1)] for n in range(near) for x in range(wide)]
     ).reshape(near * wide, far, rows, half)
     near_groups = [
         [device(f, n, c, x, y) for n in range(near) for x in range(wide)]
@@ -102,7 +99,7 @@
         gap = LANES - rest
         return jnp.sum(tile_value + jnp.pad(rest_value, ((0, 0), (0, 0), (0, gap))), axis=2)
 
-    row_part = along_rows(*squares)
+    row_part = old_rows + 0.1 * along_rows(*squares) / COLS
     scaled_part = along_rows(*(value / c for value, c in zip(power, cols)))
     sums = jnp.concatenate(
         [
@@ -110,23 +107,23 @@
             jnp.pad(param_part, (0, all_rows - rows)),
         ]
     )[None]
-    known = jnp.concatenate([jnp.pad(jnp.concatenate(cols), (0, LANES - rest)), priors])
-    known = jnp.broadcast_to(known, (slabs, 1, 2 * LANES + all_rows))
+    gap = 2 * rows
+    rest_cols = jnp.pad(cols[1], (2 * all_rows + gap, all_rows - gap - rest))[None]
+    known = jnp.broadcast_to(cols[0], (slabs, 1, LANES))
     main = gradient[:, 0, : wide * cut].reshape(deep, wide, cut).transpose(1, 0, 2)
     side = gradient[:, 0, wide * cut :].reshape(deep, wide, piece - cut).transpose(1, 0, 2)
     known = jnp.concatenate(
         [main.reshape(slabs, 1, cut), side.reshape(slabs, 1, piece - cut), known], axis=2
     )
-    sums, known = lax.optimization_barrier((sums, known))
-    sums = jnp.sum(everyone(sums, "dp", replicas), axis=0)
+    sums, known, rest_cols = lax.optimization_barrier((sums, known, rest_cols))
+    sums = jnp.sum(everyone(sums, "dp", replicas), axis=0) + rest_cols
 
     known = jnp.concatenate([known, jnp.broadcast_to(sums, (slabs, *sums.shape))], axis=2)
     known = lax.all_to_all(known, "mp", 0, 0, tiled=True)
-    at = piece + 2 * LANES
-    priors = jnp.sum(known[:, 0, at : at + all_rows], axis=0)
-    sums = jnp.sum(known[:, 0, at + all_rows :], axis=0)
-    row_sum, scaled_sum, param_sum = (sums[i * all_rows : (i + 1) * all_rows] for i in range(3))
-    row_states = 0.9 * priors + 0.1 * row_sum / COLS
+    at = piece + LANES
+    sums = jnp.sum(known[:, 0, at:], axis=0)
+    row_states, scaled_sum, param_sum = (sums[i * all_rows : (i + 1) * all_rows] for i in range(3))
+    param_sum = jnp.where(jnp.arange(all_rows) < rows, param_sum, 0.0)
     totals = jnp.stack([row_states, scaled_sum / row_states, param_sum])
     totals = lax.optimization_barrier(jnp.broadcast_to(totals[:, None, :], (3, rows, all_rows)))
     totals = jnp.sum(totals, axis=2)
@@ -137,15 +134,15 @@
         value = value.transpose(1, 0, 2).reshape(lines, wide, deep * width)
         return [value[:, x] for x in range(wide)]
 
-    def whole(start, lines):
-        tile_value = in_columns(start, LANES, lines)
-        rest_value = in_columns(start + lines * LANES, rest, lines)
+    def whole(tile_start, rest_start, lines):
+        tile_value = in_columns(tile_start, LANES, lines)
+        rest_value = in_columns(rest_start, rest, lines)
         return jnp.concatenate(
             [v for pair in zip(tile_value, rest_value) for v in pair], axis=1
         )
 
-    gradient = whole(0, rows)
-    col_state = whole(piece, 1)[0]
+    gradient = whole(0, cut, rows)
+    col_state = whole(piece, at + 2 * all_rows + gap, 1)[0]
     row_total = totals[0] / all_rows
     entries = float(all_rows * COLS)
     update_rms = jnp.sqrt(row_total * totals[1] / entries)

time: 90.1 us -> 89.5 us (level)
  transfers between devices with their start and end apart: 1 -> 1, of which waited for: 0 -> 1; matrix products, arithmetic and copies ran while one was open for 3% -> 3% of each run, Pallas kernels for 0% -> 0%
where the time goes in v5:
time: 89.5 us; the launch traced here: 89.2 us
  blocking collectives  71.4 us (80%)
  starting transfers between devices  8.79 us (10%)
  other arithmetic  4.55 us (5%)
  local copies, waits for them, and re-layouts  3.16 us (4%)
  between operations  1.14 us (1%)
    all_to_all x1, blocking collectives, on_device(): lax.all_to_all(sent, ('mp', 'dp'), 0, 0, tiled=True, axis_index_groups=fa...  24.7 us
    all_to_all x1, blocking collectives, on_device(): lax.all_to_all(both, ('mp', 'dp'), 0, 0, tiled=True, axis_index_groups=ne...  18.8 us
    all_to_all x1, blocking collectives, everyone(): return lax.all_to_all(sent, axis, 0, 0, tiled=True)  16.8 us
    all_to_all x1, blocking collectives, on_device(): known = lax.all_to_all(known, 'mp', 0, 0, tiled=True)  11.2 us
    ppermute x1, starting transfers between devices, on_device(): got = lax.ppermute(sent, 'dp', [(i, i ^ 1) for i in range(replicas)])  8.79 us
  transfers between devices with their start and end apart: 1, of which 1 were waited for; matrix products, arithmetic and copies ran while one was open for 3% of the time, Pallas kernels for 0%

profile of v5, /device:TPU:1, one launch (start us, length us, event | category | flops | bytes accessed | tf_op | source)
XLA Modules:
  0.0 89.2 jit_solution(10556840610487284519)
XLA Ops:
  0.7 1.2 %convert_bitcast_fusion = f32[16,8,2304]{2,1,0:T(8,128)S(1)} fusion(bf16[8,16,2,2304]{3,0,2,1:T(8,128)(2,1)} %bitcast.131, s32[]{:T(128)S(6)} %select_n.31), kind=kLoop, calls=%fused_computation.1 | loop fusion | flops 294912 | bytes 1769476 | tf_op jit(solution)/shard_map/convert_element_type | solution.py:35
  1.9 8.8 %collective-permute-start = (f32[16,8,2304]{2,1,0:T(8,128)S(1)}, f32[16,8,2304]{2,1,0:T(8,128)S(1)}, u32[]{:S(2)}, u32[]{:S(2)}) collective-permute-start(f32[16,8,2304]{2,1,0:T(8,128)S(1)} %convert_bitcast_fusion), channel_id=1, source_target_pairs={{0,1},{1,0},{2,3},{3,2},{4,5},{5,4},{6,7},{7,6},{8,9},{9,8},{10,11... | collective-permute-start | bytes 3538952 | tf_op jit(solution)/shard_map/ppermute | solution.py:37
  10.8 0.6 dynamic_slice.18
  11.4 0.6 dynamic_slice.17
  11.9 1.0 %multiply_reduce_fusion = f32[8]{0:T(128)S(1)} fusion(f32[8,2304]{1,0:T(8,128)} %param.5), kind=kLoop, calls=%fused_computation.25 | loop fusion | flops 36856 | bytes 73760 | tf_op jit(solution)/shard_map/reduce_sum | solution.py:47
  13.0 0.1 broadcast_select_fusion
  13.0 0.1 collective-permute-done
  13.2 0.1 bitcast_add_fusion
  13.4 18.8 %all_to_all.20 = f32[8,4,8,1152]{3,2,1,0:T(8,128)S(1)} all-to-all(f32[8,4,8,1152]{3,2,1,0:T(8,128)S(1)} %bitcast.130), channel_id=1, replica_groups={{0,256,2,258,4,260,6,262},{32,288,34,290,36,292,38,294},{64,320,66,322,..., dimensions={0} | all-to-all | bytes 2359296 | tf_op jit(solution)/shard_map/all_to_all | solution.py:63
  32.2 0.1 reduce_sum.93
  32.4 0.1 reshape.128
  32.6 0.1 reshape.129
  32.8 0.3 copy.75
  33.1 24.7 %all_to_all.21 = f32[32,1,2304]{2,1,0:T(1,128)S(1)} all-to-all(f32[32,1,2304]{2,1,0:T(1,128)S(1)} %copy.75), channel_id=1, replica_groups={{0,32,64,96,128,160,192,224,8,40,72,104,136,168,200,232,16,48,80,112,14..., dimensions={0} | all-to-all | bytes 589824 | tf_op jit(solution)/shard_map/all_to_all | solution.py:83
  57.9 0.1 mul.94
  58.1 0.1 pad.18
  58.2 0.1 reshape.132
  58.3 0.1 add_reduce_fusion.1
  58.5 0.1 add_reduce_fusion
  58.7 0.1 reshape.131
  58.8 0.1 maximum_maximum_fusion
  59.0 16.8 %all_to_all.22 = f32[32,1,384]{2,1,0:T(1,128)S(1)} all-to-all(f32[32,1,384]{2,1,0:T(1,128)S(1)} %broadcast_in_dim.63), channel_id=1, replica_groups=mesh['mp'=16,'dp'=32] {'dp'}, dimensions={0} | all-to-all | bytes 98304 | tf_op jit(solution)/shard_map/all_to_all | solution.py:12
  75.8 0.1 pad_maximum_fusion.1
  75.9 11.2 %all_to_all.23 = f32[16,1,1664]{2,1,0:T(1,128)S(1)} all-to-all(f32[16,1,1664]{2,1,0:T(1,128)S(1)} %pad_maximum_fusion.1), channel_id=1, replica_groups=mesh['mp'=16,'dp'=32] {'mp'}, dimensions={0} | all-to-all | bytes 212992 | tf_op jit(solution)/shard_map/all_to_all | solution.py:122
  87.1 0.1 slice_reduce_fusion.1
  87.2 0.1 reshape_transpose_reshape_squeeze.7
  87.4 0.1 reduce_sum.102
  87.4 0.5 fusion.12
  88.1 0.1 reshape_squeeze.19
  88.2 0.1 reshape.135
  88.3 0.1 dynamic_slice.20
  88.4 0.7 fusion.9
  (71 shorter events, 1.0 us)
Async XLA Ops:
  0.6 12.5 %copy-start = (bf16[1,8,73728]{2,1,0:T(8,128)(2,1)S(1)}, bf16[1,8,73728]{2,1,0:T(8,128)(2,1)}, u32[]{:S(2)}) copy-start(bf16[1,8,73728]{2,1,0:T(8,128)(2,1)} %param.4) | copy-start | bytes 3538948
  0.6 10.1 %copy-start.3 = (f32[2304]{0:T(1024)S(1)}, f32[2304]{0:T(1024)}, u32[]{:S(2)}) copy-start(f32[2304]{0:T(1024)} %param.7) | copy-start | bytes 27652
  0.7 12.3 %copy-start.5 = (f32[8]{0:T(128)S(1)}, f32[8]{0:T(128)}, u32[]{:S(2)}) copy-start(f32[8]{0:T(128)} %param.6) | copy-start | bytes 100
  1.9 11.2 %collective-permute-start = (f32[16,8,2304]{2,1,0:T(8,128)S(1)}, f32[16,8,2304]{2,1,0:T(8,128)S(1)}, u32[]{:S(2)}, u32[]{:S(2)}) collective-permute-start(f32[16,8,2304]{2,1,0:T(8,128)S(1)} %convert_bitcast_fusion), channel_id=1, source_target_pairs={{0,1},{1,0},{2,3},{3,2},{4,5},{5,4},{6,7},{7,6},{8,9},{9,8},{10,11... | collective-permute-start | bytes 3538952 | tf_op jit(solution)/shard_map/ppermute | solution.py:37
  32.8 25.3 %copy-start.7 = (f32[16]{0:T(128)S(1)}, f32[16]{0:T(128)}, u32[]{:S(2)}) copy-start(f32[16]{0:T(128)} %dynamic_slice.18) | copy-start | bytes 196
  33.1 25.4 %copy-start.6 = (f32[128]{0:T(128)S(1)}, f32[128]{0:T(128)}, u32[]{:S(2)}) copy-start(f32[128]{0:T(128)} %dynamic_slice.17) | copy-start | bytes 1540
  58.1 30.4 %copy-start.1 = (f32[8,2304]{1,0:T(8,128)S(1)}, f32[8,2304]{1,0:T(8,128)}, u32[]{:S(2)}) copy-start(f32[8,2304]{1,0:T(8,128)} %param.5) | copy-start | bytes 221188
  88.4 0.8 copy-start.4
  88.4 0.8 copy-start.2

commit v6 on v5

--- a/solution.py
+++ b/solution.py
@@ -146,6 +146,7 @@
     row_total = totals[0] / all_rows
     entries = float(all_rows * COLS)
     update_rms = jnp.sqrt(row_total * totals[1] / entries)
+    update_rms = lax.optimization_barrier(update_rms)
     param_rms = jnp.sqrt(totals[2] / entries + 1e-06)
     scale = 0.01 * param_rms * jnp.sqrt(row_total) / jnp.maximum(1.0, update_rms)
     update = gradient / jnp.sqrt(row_state[:, None] * col_state[None, :])

time: 89.5 us -> 89 us (level)
  no operation moved by 1% of the time
where the time goes in v6:
time: 89 us; the launch traced here: 88.7 us
  blocking collectives  71.4 us (80%)
  starting transfers between devices  8.79 us (10%)
  other arithmetic  4.05 us (5%)
  local copies, waits for them, and re-layouts  3.16 us (4%)
  between operations  1.15 us (1%)
    all_to_all x1, blocking collectives, on_device(): lax.all_to_all(sent, ('mp', 'dp'), 0, 0, tiled=True, axis_index_groups=fa...  24.7 us
    all_to_all x1, blocking collectives, on_device(): lax.all_to_all(both, ('mp', 'dp'), 0, 0, tiled=True, axis_index_groups=ne...  18.8 us
    all_to_all x1, blocking collectives, everyone(): return lax.all_to_all(sent, axis, 0, 0, tiled=True)  16.8 us
    all_to_all x1, blocking collectives, on_device(): known = lax.all_to_all(known, 'mp', 0, 0, tiled=True)  11.2 us
    ppermute x1, starting transfers between devices, on_device(): got = lax.ppermute(sent, 'dp', [(i, i ^ 1) for i in range(replicas)])  8.79 us
  transfers between devices with their start and end apart: 1, of which 1 were waited for; matrix products, arithmetic and copies ran while one was open for 3% of the time, Pallas kernels for 0%

profile of v6, /device:TPU:1, one launch (start us, length us, event | category | flops | bytes accessed | tf_op | source)
XLA Modules:
  0.0 88.7 jit_solution(13531069345953753193)
XLA Ops:
  0.7 1.2 %convert_bitcast_fusion = f32[16,8,2304]{2,1,0:T(8,128)S(1)} fusion(bf16[8,16,2,2304]{3,0,2,1:T(8,128)(2,1)} %bitcast.133, s32[]{:T(128)S(6)} %select_n.31), kind=kLoop, calls=%fused_computation.1 | loop fusion | flops 294912 | bytes 1769476 | tf_op jit(solution)/shard_map/convert_element_type | solution.py:35
  1.9 8.8 %collective-permute-start = (f32[16,8,2304]{2,1,0:T(8,128)S(1)}, f32[16,8,2304]{2,1,0:T(8,128)S(1)}, u32[]{:S(2)}, u32[]{:S(2)}) collective-permute-start(f32[16,8,2304]{2,1,0:T(8,128)S(1)} %convert_bitcast_fusion), channel_id=1, source_target_pairs={{0,1},{1,0},{2,3},{3,2},{4,5},{5,4},{6,7},{7,6},{8,9},{9,8},{10,11... | collective-permute-start | bytes 3538952 | tf_op jit(solution)/shard_map/ppermute | solution.py:37
  10.8 0.6 dynamic_slice.18
  11.4 0.6 dynamic_slice.17
  11.9 1.0 %multiply_reduce_fusion = f32[8]{0:T(128)S(1)} fusion(f32[8,2304]{1,0:T(8,128)} %param.5), kind=kLoop, calls=%fused_computation.25 | loop fusion | flops 36856 | bytes 73760 | tf_op jit(solution)/shard_map/reduce_sum | solution.py:47
  13.0 0.1 broadcast_select_fusion
  13.0 0.1 collective-permute-done
  13.2 0.1 bitcast_add_fusion
  13.4 18.8 %all_to_all.20 = f32[8,4,8,1152]{3,2,1,0:T(8,128)S(1)} all-to-all(f32[8,4,8,1152]{3,2,1,0:T(8,128)S(1)} %bitcast.132), channel_id=1, replica_groups={{0,256,2,258,4,260,6,262},{32,288,34,290,36,292,38,294},{64,320,66,322,..., dimensions={0} | all-to-all | bytes 2359296 | tf_op jit(solution)/shard_map/all_to_all | solution.py:63
  32.2 0.1 reduce_sum.93
  32.4 0.1 reshape.103
  32.6 0.1 reshape.104
  32.8 0.3 copy.75
  33.1 24.7 %all_to_all.21 = f32[32,1,2304]{2,1,0:T(1,128)S(1)} all-to-all(f32[32,1,2304]{2,1,0:T(1,128)S(1)} %copy.75), channel_id=1, replica_groups={{0,32,64,96,128,160,192,224,8,40,72,104,136,168,200,232,16,48,80,112,14..., dimensions={0} | all-to-all | bytes 589824 | tf_op jit(solution)/shard_map/all_to_all | solution.py:83
  57.9 0.1 mul.82
  58.1 0.1 pad.18
  58.2 0.1 reshape.107
  58.3 0.1 add_reduce_fusion.1
  58.5 0.1 add_reduce_fusion
  58.6 0.1 copy.78
  58.7 0.1 reshape.106
  58.8 0.1 maximum_maximum_fusion
  59.0 16.8 %all_to_all.22 = f32[32,1,384]{2,1,0:T(1,128)S(1)} all-to-all(f32[32,1,384]{2,1,0:T(1,128)S(1)} %broadcast_in_dim.63), channel_id=1, replica_groups=mesh['mp'=16,'dp'=32] {'dp'}, dimensions={0} | all-to-all | bytes 98304 | tf_op jit(solution)/shard_map/all_to_all | solution.py:12
  75.8 0.1 pad_maximum_fusion.1
  75.9 11.2 %all_to_all.23 = f32[16,1,1664]{2,1,0:T(1,128)S(1)} all-to-all(f32[16,1,1664]{2,1,0:T(1,128)S(1)} %pad_maximum_fusion.1), channel_id=1, replica_groups=mesh['mp'=16,'dp'=32] {'mp'}, dimensions={0} | all-to-all | bytes 212992 | tf_op jit(solution)/shard_map/all_to_all | solution.py:122
  87.1 0.1 slice_reduce_fusion.1
  87.2 0.1 reshape_transpose_reshape_squeeze.7
  87.4 0.1 reduce_sum.102
  87.6 0.1 reshape_squeeze.19
  87.7 0.1 reshape.110
  87.8 0.1 dynamic_slice.20
  87.9 0.7 fusion.9
  (74 shorter events, 1.0 us)
Async XLA Ops:
  0.6 12.5 %copy-start = (bf16[1,8,73728]{2,1,0:T(8,128)(2,1)S(1)}, bf16[1,8,73728]{2,1,0:T(8,128)(2,1)}, u32[]{:S(2)}) copy-start(bf16[1,8,73728]{2,1,0:T(8,128)(2,1)} %param.4) | copy-start | bytes 3538948
  0.6 10.1 %copy-start.3 = (f32[2304]{0:T(1024)S(1)}, f32[2304]{0:T(1024)}, u32[]{:S(2)}) copy-start(f32[2304]{0:T(1024)} %param.7) | copy-start | bytes 27652
  0.7 12.3 %copy-start.6 = (f32[8]{0:T(128)S(1)}, f32[8]{0:T(128)}, u32[]{:S(2)}) copy-start(f32[8]{0:T(128)} %param.6) | copy-start | bytes 100
  1.9 11.2 %collective-permute-start = (f32[16,8,2304]{2,1,0:T(8,128)S(1)}, f32[16,8,2304]{2,1,0:T(8,128)S(1)}, u32[]{:S(2)}, u32[]{:S(2)}) collective-permute-start(f32[16,8,2304]{2,1,0:T(8,128)S(1)} %convert_bitcast_fusion), channel_id=1, source_target_pairs={{0,1},{1,0},{2,3},{3,2},{4,5},{5,4},{6,7},{7,6},{8,9},{9,8},{10,11... | collective-permute-start | bytes 3538952 | tf_op jit(solution)/shard_map/ppermute | solution.py:37
  32.8 25.3 %copy-start.8 = (f32[16]{0:T(128)S(1)}, f32[16]{0:T(128)}, u32[]{:S(2)}) copy-start(f32[16]{0:T(128)} %dynamic_slice.18) | copy-start | bytes 196
  33.1 25.4 %copy-start.7 = (f32[128]{0:T(128)S(1)}, f32[128]{0:T(128)}, u32[]{:S(2)}) copy-start(f32[128]{0:T(128)} %dynamic_slice.17) | copy-start | bytes 1540
  58.1 29.9 %copy-start.1 = (f32[8,2304]{1,0:T(8,128)S(1)}, f32[8,2304]{1,0:T(8,128)}, u32[]{:S(2)}) copy-start(f32[8,2304]{1,0:T(8,128)} %param.5) | copy-start | bytes 221188
  87.5 1.2 %copy-start.5 = (f32[8]{0:T(128)}, f32[8]{0:T(128)S(1)}, u32[]{:S(2)}) copy-start(f32[8]{0:T(128)S(1)} %sqrt_bitcast_fusion) | copy-start | bytes 100
  87.9 0.8 copy-start.4
  87.9 0.8 copy-start.2

commit v7 on v6

--- a/solution.py
+++ b/solution.py
@@ -36,7 +36,8 @@
     kept = lax.dynamic_index_in_dim(blocks, core, 0, keepdims=False)
     got = lax.ppermute(sent, "dp", [(i, i ^ 1) for i in range(replicas)])
     place = wide * along + across
-    first_row = (place * rows).astype(jnp.uint32)
+    lines = jnp.arange(rows)[:, None] + place * rows
+    own_lane = jnp.where(jnp.arange(all_rows)[None, :] == lines, 1.0, 0.0)
     old_part = lax.optimization_barrier(0.9 * col_prior)
     tile_at = half * across + LANES * along
     rest_at = half * across + tiles + rest * along
@@ -45,8 +46,8 @@
     own_slab = jnp.arange(slabs)[:, None] == place
     old_rows = jnp.where(own_slab, (0.9 * row_prior / replicas)[None, :], 0.0)
     param_part = jnp.sum(param * param, axis=1)
-    got, param_part, old_rows, tile_old, rest_old, first_row = lax.optimization_barrier(
-        (got, param_part, old_rows, tile_old, rest_old, first_row)
+    got, param_part, old_rows, tile_old, rest_old, own_lane = lax.optimization_barrier(
+        (got, param_part, old_rows, tile_old, rest_old, own_lane)
     )
     both = kept.astype(jnp.float32) + got
 
@@ -126,8 +127,8 @@
     param_sum = jnp.where(jnp.arange(all_rows) < rows, param_sum, 0.0)
     totals = jnp.stack([row_states, scaled_sum / row_states, param_sum])
     totals = lax.optimization_barrier(jnp.broadcast_to(totals[:, None, :], (3, rows, all_rows)))
+    row_state = jnp.sum(jnp.where(own_lane > 0.0, totals[0], 0.0), axis=1)
     totals = jnp.sum(totals, axis=2)
-    row_state = lax.dynamic_slice(row_states, (first_row,), (rows,))
 
     def in_columns(start, width, lines):
         value = known[:, 0, start : start + lines * width].reshape(slabs, lines, width)

time: 89 us -> 89 us (level)
  transfers between devices with their start and end apart: 1 -> 1, of which waited for: 1 -> 0; matrix products, arithmetic and copies ran while one was open for 3% -> 3% of each run, Pallas kernels for 0% -> 0%
where the time goes in v7:
time: 89 us; the launch traced here: 88.7 us
  blocking collectives  71.4 us (80%)
  starting transfers between devices  8.79 us (10%)
  other arithmetic  4.24 us (5%)
  local copies, waits for them, and re-layouts  3.09 us (3%)
  between operations  1.17 us (1%)
    all_to_all x1, blocking collectives, on_device(): lax.all_to_all(sent, ('mp', 'dp'), 0, 0, tiled=True, axis_index_groups=fa...  24.7 us
    all_to_all x1, blocking collectives, on_device(): lax.all_to_all(both, ('mp', 'dp'), 0, 0, tiled=True, axis_index_groups=ne...  18.8 us
    all_to_all x1, blocking collectives, everyone(): return lax.all_to_all(sent, axis, 0, 0, tiled=True)  16.7 us
    all_to_all x1, blocking collectives, on_device(): known = lax.all_to_all(known, 'mp', 0, 0, tiled=True)  11.2 us
    ppermute x1, starting transfers between devices, on_device(): got = lax.ppermute(sent, 'dp', [(i, i ^ 1) for i in range(replicas)])  8.79 us
  transfers between devices with their start and end apart: 1, of which 0 were waited for; matrix products, arithmetic and copies ran while one was open for 3% of the time, Pallas kernels for 0%

profile of v7, /device:TPU:1, one launch (start us, length us, event | category | flops | bytes accessed | tf_op | source)
XLA Modules:
  0.0 88.7 jit_solution(10233939986023949124)
XLA Ops:
  0.7 1.2 %convert_bitcast_fusion = f32[16,8,2304]{2,1,0:T(8,128)S(1)} fusion(bf16[8,16,2,2304]{3,0,2,1:T(8,128)(2,1)} %bitcast.139, s32[]{:T(128)S(6)} %select_n.39), kind=kLoop, calls=%fused_computation.1 | loop fusion | flops 294912 | bytes 1769476 | tf_op jit(solution)/shard_map/convert_element_type | solution.py:35
  1.9 8.8 %collective-permute-start = (f32[16,8,2304]{2,1,0:T(8,128)S(1)}, f32[16,8,2304]{2,1,0:T(8,128)S(1)}, u32[]{:S(2)}, u32[]{:S(2)}) collective-permute-start(f32[16,8,2304]{2,1,0:T(8,128)S(1)} %convert_bitcast_fusion), channel_id=1, source_target_pairs={{0,1},{1,0},{2,3},{3,2},{4,5},{5,4},{6,7},{7,6},{8,9},{9,8},{10,11... | collective-permute-start | bytes 3538952 | tf_op jit(solution)/shard_map/ppermute | solution.py:37
  10.8 0.6 dynamic_slice.15
  11.4 0.6 dynamic_slice.14
  11.9 1.0 %multiply_reduce_fusion = f32[8]{0:T(128)S(1)} fusion(f32[8,2304]{1,0:T(8,128)} %param.5), kind=kLoop, calls=%fused_computation.25 | loop fusion | flops 36856 | bytes 73760 | tf_op jit(solution)/shard_map/reduce_sum | solution.py:48
  13.0 0.1 fusion.12
  13.0 0.1 broadcast_select_fusion
  13.2 0.1 bitcast_add_fusion
  13.4 18.8 %all_to_all.20 = f32[8,4,8,1152]{3,2,1,0:T(8,128)S(1)} all-to-all(f32[8,4,8,1152]{3,2,1,0:T(8,128)S(1)} %bitcast.138), channel_id=1, replica_groups={{0,256,2,258,4,260,6,262},{32,288,34,290,36,292,38,294},{64,320,66,322,..., dimensions={0} | all-to-all | bytes 2359296 | tf_op jit(solution)/shard_map/all_to_all | solution.py:64
  32.2 0.1 reduce_sum.102
  32.4 0.1 reshape.108
  32.6 0.1 reshape.109
  32.8 0.3 copy.75
  33.1 24.7 %all_to_all.21 = f32[32,1,2304]{2,1,0:T(1,128)S(1)} all-to-all(f32[32,1,2304]{2,1,0:T(1,128)S(1)} %copy.75), channel_id=1, replica_groups={{0,32,64,96,128,160,192,224,8,40,72,104,136,168,200,232,16,48,80,112,14..., dimensions={0} | all-to-all | bytes 589824 | tf_op jit(solution)/shard_map/all_to_all | solution.py:84
  57.9 0.1 mul.82
  58.1 0.1 pad.18
  58.2 0.1 reshape.112
  58.3 0.1 add_reduce_fusion.1
  58.4 0.1 add_reduce_fusion
  58.6 0.1 copy.78
  58.7 0.1 reshape.111
  58.8 0.1 maximum_maximum_fusion
  59.0 16.7 %all_to_all.22 = f32[32,1,384]{2,1,0:T(1,128)S(1)} all-to-all(f32[32,1,384]{2,1,0:T(1,128)S(1)} %broadcast_in_dim.77), channel_id=1, replica_groups=mesh['mp'=16,'dp'=32] {'dp'}, dimensions={0} | all-to-all | bytes 98304 | tf_op jit(solution)/shard_map/all_to_all | solution.py:12
  75.8 0.1 pad_maximum_fusion.1
  75.9 11.2 %all_to_all.23 = f32[16,1,1664]{2,1,0:T(1,128)S(1)} all-to-all(f32[16,1,1664]{2,1,0:T(1,128)S(1)} %pad_maximum_fusion.1), channel_id=1, replica_groups=mesh['mp'=16,'dp'=32] {'mp'}, dimensions={0} | all-to-all | bytes 212992 | tf_op jit(solution)/shard_map/all_to_all | solution.py:123
  87.1 0.1 slice_reduce_fusion.1
  87.2 0.1 reshape_transpose_reshape_squeeze.7
  87.3 0.1 reduce_sum.111
  87.4 0.1 fusion.11
  87.7 0.1 reshape_squeeze.19
  87.8 0.1 reshape.115
  88.0 0.7 fusion.9
  (76 shorter events, 1.0 us)
Async XLA Ops:
  0.6 12.5 %copy-start = (bf16[1,8,73728]{2,1,0:T(8,128)(2,1)S(1)}, bf16[1,8,73728]{2,1,0:T(8,128)(2,1)}, u32[]{:S(2)}) copy-start(bf16[1,8,73728]{2,1,0:T(8,128)(2,1)} %param.4) | copy-start | bytes 3538948
  0.6 10.1 %copy-start.3 = (f32[2304]{0:T(1024)S(1)}, f32[2304]{0:T(1024)}, u32[]{:S(2)}) copy-start(f32[2304]{0:T(1024)} %param.7) | copy-start | bytes 27652
  0.7 12.3 %copy-start.6 = (f32[8]{0:T(128)S(1)}, f32[8]{0:T(128)}, u32[]{:S(2)}) copy-start(f32[8]{0:T(128)} %param.6) | copy-start | bytes 100
  1.9 11.2 %collective-permute-start = (f32[16,8,2304]{2,1,0:T(8,128)S(1)}, f32[16,8,2304]{2,1,0:T(8,128)S(1)}, u32[]{:S(2)}, u32[]{:S(2)}) collective-permute-start(f32[16,8,2304]{2,1,0:T(8,128)S(1)} %convert_bitcast_fusion), channel_id=1, source_target_pairs={{0,1},{1,0},{2,3},{3,2},{4,5},{5,4},{6,7},{7,6},{8,9},{9,8},{10,11... | collective-permute-start | bytes 3538952 | tf_op jit(solution)/shard_map/ppermute | solution.py:37
  32.8 25.2 %copy-start.8 = (f32[16]{0:T(128)S(1)}, f32[16]{0:T(128)}, u32[]{:S(2)}) copy-start(f32[16]{0:T(128)} %dynamic_slice.15) | copy-start | bytes 196
  33.1 25.3 %copy-start.7 = (f32[128]{0:T(128)S(1)}, f32[128]{0:T(128)}, u32[]{:S(2)}) copy-start(f32[128]{0:T(128)} %dynamic_slice.14) | copy-start | bytes 1540
  58.0 29.9 %copy-start.1 = (f32[8,2304]{1,0:T(8,128)S(1)}, f32[8,2304]{1,0:T(8,128)}, u32[]{:S(2)}) copy-start(f32[8,2304]{1,0:T(8,128)} %param.5) | copy-start | bytes 221188
  87.5 1.2 %copy-start.4 = (f32[8]{0:T(128)}, f32[8]{0:T(128)S(1)}, u32[]{:S(2)}) copy-start(f32[8]{0:T(128)S(1)} %fusion.11) | copy-start | bytes 100
  87.5 1.1 %copy-start.5 = (f32[8]{0:T(128)}, f32[8]{0:T(128)S(1)}, u32[]{:S(2)}) copy-start(f32[8]{0:T(128)S(1)} %sqrt_bitcast_fusion) | copy-start | bytes 100
  87.9 0.8 copy-start.2
